TPU v7x, 32 devices: a whole 2x2x4 slice. The times are simulated.
32 devices in a mesh: groups: 2 (over x), seq: 16 (over z, y, core).
Axes of the slice: x: 2, y: 2, z: 4, core: 2. Of those that a mesh axis runs over, the one named last changes fastest.
Arguments:
- queries: bfloat16 [8, 4096, 3072], P('groups', 'seq'), parts along dimension 0, may hold values from -28 to 28
- keys: bfloat16 [8, 4096, 3072], P('groups', 'seq'), parts along dimension 0, may hold values from -28 to 28
- values: bfloat16 [8, 4096, 3072], P('groups', 'seq'), parts along dimension 0, may hold values from -6 to 6
- tile_list: int32 [24, 16, 16], P(None, 'seq'), may hold values from 0 to 15, as said below
- head_counts: int32 [24], replicated, may hold values from 4 to 16
Outputs:
- attended: bfloat16 [8, 4096, 3072], P('groups', 'seq'), parts along dimension 0
There are 2 independent parts, one for each index of `groups`. A program takes and returns all parts, laid end to end along the dimension named above; an argument that names none is the same for every part. Nothing has to cross between parts.
Inputs may be any that keep to these rules, and one draw needn't show every extreme that they name: `tile_list`: slot 0 of every list is the query tile itself; the 16 slots of a list name distinct tiles.
All inputs are finite; a program needn't handle non-finite values.
Results may differ from a plain program's by a relative error of at most 0.0047.
Values may be sent and summed in bfloat16 or wider, within the bound.
A program may use at most 192 MiB of HBM per device.

v0:
```python
import functools

import jax
import jax.numpy as jnp
from jax import lax
from jax.experimental import pallas as pl
from jax.experimental.pallas import tpu as pltpu
from jax.sharding import PartitionSpec as P

GROUP = 4
CHUNKS = 3
LOG2E = 1.4426950408889634


def place(p, j, devices):
    return j * devices + (p if j % 2 == 0 else devices - 1 - p)


def pack_kernel(slots, reqs, order, queries, keys, values, out, sem):
    devices = out.shape[0]
    length, width = out.shape[3:]
    copies = []
    for here, j in enumerate(slots):
        for p in range(devices):
            rank = place(p, j, devices)
            head = order[rank // reqs]
            columns = pl.ds(pl.multiple_of(head * width, width), width)
            for which, array in enumerate((queries, keys, values)):
                copies.append(
                    pltpu.make_async_copy(
                        array.at[rank % reqs, :, columns],
                        out.at[p, here, which],
                        sem.at[len(copies)],
                    )
                )
    for copy in copies:
        copy.start()
    for copy in copies:
        copy.wait()


def unpack_kernel(chunks, reqs, order, *refs):
    arrays, out, sem = refs[: len(chunks)], refs[-2], refs[-1]
    devices, _, length, width = arrays[0].shape
    copies = []
    for slots, array in zip(chunks, arrays):
        for here, j in enumerate(slots):
            for p in range(devices):
                rank = place(p, j, devices)
                head = order[rank // reqs]
                columns = pl.ds(pl.multiple_of(head * width, width), width)
                copies.append(
                    pltpu.make_async_copy(
                        array.at[p, here],
                        out.at[rank % reqs, :, columns],
                        sem.at[len(copies)],
                    )
                )
    for copy in copies:
        copy.start()
    for copy in copies:
        copy.wait()


def attend_kernel(window, owned, counts, lists, data, out, turned):
    tiles = data.shape[0]
    rows, width = data.shape[3:]
    head = owned[pl.program_id(0)]
    count = counts[head]
    group = GROUP if tiles % GROUP == 0 else 1
    factor = width ** (-0.5) * LOG2E

    @pl.loop(0, tiles)
    def turn(tile):
        turned[tile, :width, :] = data[tile, 0, 2].T
        turned[tile, width:, :] = jnp.ones((16, rows), jnp.bfloat16)

    @pl.loop(0, tiles // group)
    def some_tiles(block):
        first = block * group
        bases = [(head * tiles + first + g) * window for g in range(group)]

        def advance(slot, carry):
            result = []
            for g in range(group):
                running, accum = carry[g]
                picked = lists[bases[g] + slot]
                scores = lax.dot_general(
                    data[picked, 0, 1],
                    data[first + g, 0, 0],
                    (((1,), (1,)), ((), ())),
                    preferred_element_type=jnp.float32,
                )
                newmax = jnp.maximum(running, jnp.max(scores, axis=0, keepdims=True) * factor)
                carried = jnp.exp2(running - newmax)
                weights = jnp.exp2(scores * factor - newmax).astype(jnp.bfloat16)
                accum = carried * accum + jnp.dot(
                    turned[picked], weights, preferred_element_type=jnp.float32
                )
                result.append((newmax, accum))
            return tuple(result)

        start = tuple(
            (
                jnp.full((1, rows), -1e30, jnp.float32),
                jnp.zeros((width + 16, rows), jnp.float32),
            )
            for _ in range(group)
        )
        done = lax.fori_loop(0, count, advance, start)
        for g in range(group):
            accum = done[g][1]
            ratio = accum[:width] / accum[width : width + 1]
            out[first + g, 0] = ratio.T.astype(jnp.bfloat16)


def on_device(queries, keys, values, tile_list, head_counts):
    reqs, rows, model_width = queries.shape
    heads = head_counts.shape[0]
    window = tile_list.shape[2]
    width = model_width // heads
    devices = lax.axis_size("seq")
    tasks = reqs * heads
    per_device = tasks // devices
    me = lax.axis_index("seq")
    each = -(-per_device // CHUNKS)
    chunks = [
        tuple(range(begin, min(begin + each, per_device)))
        for begin in range(0, per_device, each)
    ]

    ids = jnp.arange(heads, dtype=jnp.int32)
    mine, other = head_counts[:, None], head_counts[None, :]
    ahead = (other > mine) | ((other == mine) & (ids[None, :] < ids[:, None]))
    ranks = jnp.sum(ahead.astype(jnp.int32), axis=1)
    order = jnp.sum(jnp.where(ranks[None, :] == ids[:, None], ids[None, :], 0), axis=1)

    lists = lax.all_gather(tile_list, "seq", axis=1, tiled=True).reshape(-1)

    smem = pl.BlockSpec(memory_space=pltpu.SMEM)
    hbm = pl.BlockSpec(memory_space=pl.ANY)
    arrived = []
    for slots in chunks:
        packed = pl.pallas_call(
            functools.partial(pack_kernel, slots, reqs),
            out_shape=jax.ShapeDtypeStruct((devices, len(slots), 3, rows, width), jnp.bfloat16),
            in_specs=[smem, hbm, hbm, hbm],
            out_specs=hbm,
            scratch_shapes=[pltpu.SemaphoreType.DMA((3 * devices * len(slots),))],
        )(order, queries, keys, values)
        arrived.append(lax.all_to_all(packed, "seq", split_axis=0, concat_axis=0, tiled=True))

    returned = []
    for slots, data in zip(chunks, arrived):
        spots = jnp.stack(
            [place(me, j, devices) // reqs for j in slots]
        )
        owned = jnp.sum(jnp.where(spots[:, None] == ids[None, :], order[None, :], 0), axis=1)
        count = len(slots)
        done = pl.pallas_call(
            functools.partial(attend_kernel, window),
            out_shape=jax.ShapeDtypeStruct((devices, count, rows, width), jnp.bfloat16),
            grid_spec=pltpu.PrefetchScalarGridSpec(
                num_scalar_prefetch=3,
                grid=(count,),
                in_specs=[
                    pl.BlockSpec((devices, 1, 3, rows, width), lambda i, *_: (0, i, 0, 0, 0))
                ],
                out_specs=pl.BlockSpec((devices, 1, rows, width), lambda i, *_: (0, i, 0, 0)),
                scratch_shapes=[pltpu.VMEM((devices, width + 16, rows), jnp.bfloat16)],
            ),
            compiler_params=pltpu.CompilerParams(vmem_limit_bytes=40 * 1024 * 1024),
            cost_estimate=pl.CostEstimate(
                flops=count * devices * 10 * 4 * rows * rows * width,
                bytes_accessed=count * devices * 4 * rows * width * 2,
                transcendentals=count * devices * 10 * rows * rows,
            ),
        )(owned, head_counts, lists, data)
        returned.append(lax.all_to_all(done, "seq", split_axis=0, concat_axis=0, tiled=True))

    return pl.pallas_call(
        functools.partial(unpack_kernel, chunks, reqs),
        out_shape=jax.ShapeDtypeStruct(queries.shape, jnp.bfloat16),
        in_specs=[smem] + [hbm] * len(chunks),
        out_specs=hbm,
        scratch_shapes=[pltpu.SemaphoreType.DMA((tasks,))],
    )(order, *returned)


def solution(mesh):
    in_specs = (
        P("groups", "seq", None),
        P("groups", "seq", None),
        P("groups", "seq", None),
        P(None, "seq", None),
        P(),
    )
    out_specs = P("groups", "seq", None)
    return jax.shard_map(
        on_device, mesh=mesh, in_specs=in_specs, out_specs=out_specs, check_vma=False
    )
```

profile of v0, /device:TPU:1, one launch (start us, length us, event | category | flops | bytes accessed | tf_op | source)
XLA Modules:
  0.0 1336.7 jit_solution(17965019290170310476)
XLA Ops:
  0.0 0.9 convert_reduce_fusion
  0.9 0.6 select_reduce_fusion.order
  1.5 193.2 %shard_map.59 = bf16[16,2,3,256,128]{4,3,2,1,0:T(8,128)(2,1)} custom-call(s32[24]{0:T(128)} %select_reduce_fusion.order, bf16[4,256,3072]{2,1,0:T(8,128)(2,1)} %queries.5, bf16[4,256,3072]{2,1,0:T(8,128)(2,1)} %keys.5, bf16[4,256,3072]{2,1,0:T(8,128)(2,1)} %values.5), custom_call_target="tpu_custom_call" | custom-call | tf_op jit(solution)/shard_map/pallas_call | solution.py:144
  194.8 7.4 all-to-all-start.4
  202.1 193.2 %shard_map.57 = bf16[16,2,3,256,128]{4,3,2,1,0:T(8,128)(2,1)} custom-call(s32[24]{0:T(128)} %select_reduce_fusion.order, bf16[4,256,3072]{2,1,0:T(8,128)(2,1)} %queries.5, bf16[4,256,3072]{2,1,0:T(8,128)(2,1)} %keys.5, bf16[4,256,3072]{2,1,0:T(8,128)(2,1)} %values.5), custom_call_target="tpu_custom_call" | custom-call | tf_op jit(solution)/shard_map/pallas_call | solution.py:144
  395.3 0.0 all-to-all-done.4.data
  395.3 6.0 all-to-all-start.2
  401.4 193.2 %shard_map.55 = bf16[16,2,3,256,128]{4,3,2,1,0:T(8,128)(2,1)} custom-call(s32[24]{0:T(128)} %select_reduce_fusion.order, bf16[4,256,3072]{2,1,0:T(8,128)(2,1)} %queries.5, bf16[4,256,3072]{2,1,0:T(8,128)(2,1)} %keys.5, bf16[4,256,3072]{2,1,0:T(8,128)(2,1)} %values.5), custom_call_target="tpu_custom_call" | custom-call | tf_op jit(solution)/shard_map/pallas_call | solution.py:144
  594.6 0.0 copy-start.3
  594.6 0.0 copy-start.2
  594.6 0.0 copy-start
  594.6 0.0 all-to-all-done.2.data
  594.6 6.0 all-to-all-start
  600.7 0.0 copy-done.3
  600.7 126.8 %all_gather.3 = s32[24,16,16]{0,2,1:T(8,128)S(1)} all-gather(s32[24,1,16]{0,2,1:T(8,128)S(1)} %copy-done.3), channel_id=1, replica_groups=mesh['groups'=2,'seq'=16] {'seq'}, dimensions={1}, use_global_device_ids=true | all-gather | bytes 26112 | tf_op jit(solution)/shard_map/all_gather | solution.py:138
  727.4 0.1 copy.8
  727.6 0.1 reshape.10.lists
  727.7 0.1 pad_add_fusion.2
  727.8 0.1 pad_add_fusion
  727.9 0.0 copy-done.2
  727.9 0.2 fusion.4
  728.1 0.0 copy-done
  728.1 70.0 %shard_map.60 = bf16[16,2,256,128]{3,2,1,0:T(8,128)(2,1)} custom-call(s32[2]{0:T(128)S(1)} %get-tuple-element.5.owned, s32[24]{0:T(128)S(1)} %copy-done, s32[6144]{0:T(1024)S(1)} %reshape.10.lists, bf16[16,2,3,256,128]{4,3,2,1,0:T(8,128)(2,1)} %all-to-all-done.4.data), custom_call_target="tpu_custom_call" | custom-call | flops 10737418240 | bytes 8388608 | tf_op jit(solution)/shard_map/pallas_call | solution.py:160
  798.1 0.0 all-to-all-done.data
  798.1 25.5 %all-to-all-start.5 = ((bf16[16,2,256,128]{3,2,1,0:T(8,128)(2,1)}), bf16[16,2,256,128]{3,2,1,0:T(8,128)(2,1)S(1)}, u32[]{:S(2)}, u32[]{:S(2)}) async-start(bf16[16,2,256,128]{3,2,1,0:T(8,128)(2,1)} %shard_map.60), calls=%async_computation.5 | async-start | bytes 4194304 | tf_op jit(solution)/shard_map/all_to_all | solution.py:179
  823.5 109.3 %shard_map.58 = bf16[16,2,256,128]{3,2,1,0:T(8,128)(2,1)} custom-call(s32[2]{0:T(128)S(1)} %get-tuple-element.6.owned, s32[24]{0:T(128)S(1)} %copy-done, s32[6144]{0:T(1024)S(1)} %reshape.10.lists, bf16[16,2,3,256,128]{4,3,2,1,0:T(8,128)(2,1)} %all-to-all-done.2.data), custom_call_target="tpu_custom_call" | custom-call | flops 10737418240 | bytes 8388608 | tf_op jit(solution)/shard_map/pallas_call | solution.py:160
  932.9 0.0 all-to-all-done.5.refs_2_
  932.9 0.0 copy-start.1
  932.9 6.0 all-to-all-start.3
  938.9 0.0 copy-done.1
  938.9 153.5 %shard_map.56 = bf16[16,2,256,128]{3,2,1,0:T(8,128)(2,1)S(1)} custom-call(s32[2]{0:T(128)S(1)} %get-tuple-element.7.owned, s32[24]{0:T(128)S(1)} %copy-done, s32[6144]{0:T(1024)S(1)} %reshape.10.lists, bf16[16,2,3,256,128]{4,3,2,1,0:T(8,128)(2,1)} %all-to-all-done.data), custom_call_target="tpu_custom_call" | custom-call | flops 10737418240 | bytes 8388608 | tf_op jit(solution)/shard_map/pallas_call | solution.py:160
  1092.4 0.0 all-to-all-done.3.refs_1_
  1092.4 51.0 %all_to_all.30.refs_0_ = bf16[16,2,256,128]{3,2,1,0:T(8,128)(2,1)} all-to-all(bf16[16,2,256,128]{3,2,1,0:T(8,128)(2,1)S(1)} %shard_map.56), channel_id=1, replica_groups=mesh['groups'=2,'seq'=16] {'seq'}, dimensions={0} | all-to-all | bytes 4194304 | tf_op jit(solution)/shard_map/all_to_all | solution.py:179
  1143.4 193.2 %shard_map.61 = bf16[4,256,3072]{2,1,0:T(8,128)(2,1)} custom-call(s32[24]{0:T(128)} %select_reduce_fusion.order, bf16[16,2,256,128]{3,2,1,0:T(8,128)(2,1)} %all_to_all.30.refs_0_, bf16[16,2,256,128]{3,2,1,0:T(8,128)(2,1)} %all-to-all-done.3.refs_1_, bf16[16,2,256,128]{3,2,1,0:T(8,128)(2,1)} %copy-done.1), custom_call_target="tpu_custom_call" | custom-call | tf_op jit(solution)/shard_map/pallas_call | solution.py:181
Async XLA Ops:
  194.8 200.6 %all-to-all-start.4 = ((bf16[16,2,3,256,128]{4,3,2,1,0:T(8,128)(2,1)}), bf16[16,2,3,256,128]{4,3,2,1,0:T(8,128)(2,1)}, u32[]{:S(2)}, u32[]{:S(2)}) async-start(bf16[16,2,3,256,128]{4,3,2,1,0:T(8,128)(2,1)} %shard_map.59), calls=%async_computation.4 | async-start | bytes 12582912 | tf_op jit(solution)/shard_map/all_to_all | solution.py:151
  395.3 199.3 %all-to-all-start.2 = ((bf16[16,2,3,256,128]{4,3,2,1,0:T(8,128)(2,1)}), bf16[16,2,3,256,128]{4,3,2,1,0:T(8,128)(2,1)}, u32[]{:S(2)}, u32[]{:S(2)}) async-start(bf16[16,2,3,256,128]{4,3,2,1,0:T(8,128)(2,1)} %shard_map.57), calls=%async_computation.2 | async-start | bytes 12582912 | tf_op jit(solution)/shard_map/all_to_all | solution.py:151
  594.6 6.1 copy-start.3
  594.6 133.2 %copy-start.2 = (s32[24]{0:T(128)S(1)}, s32[24]{0:T(128)}, u32[]{:S(2)}) copy-start(s32[24]{0:T(128)} %select_reduce_fusion.order) | copy-start | bytes 292
  594.6 133.5 %copy-start = (s32[24]{0:T(128)S(1)}, s32[24]{0:T(128)}, u32[]{:S(2)}) copy-start(s32[24]{0:T(128)} %counts.5) | copy-start | bytes 292
  594.6 203.4 %all-to-all-start = ((bf16[16,2,3,256,128]{4,3,2,1,0:T(8,128)(2,1)}), bf16[16,2,3,256,128]{4,3,2,1,0:T(8,128)(2,1)}, u32[]{:S(2)}, u32[]{:S(2)}) async-start(bf16[16,2,3,256,128]{4,3,2,1,0:T(8,128)(2,1)} %shard_map.55), calls=%async_computation | async-start | bytes 12582912 | tf_op jit(solution)/shard_map/all_to_all | solution.py:151
  798.1 134.8 %all-to-all-start.5 = ((bf16[16,2,256,128]{3,2,1,0:T(8,128)(2,1)}), bf16[16,2,256,128]{3,2,1,0:T(8,128)(2,1)S(1)}, u32[]{:S(2)}, u32[]{:S(2)}) async-start(bf16[16,2,256,128]{3,2,1,0:T(8,128)(2,1)} %shard_map.60), calls=%async_computation.5 | async-start | bytes 4194304 | tf_op jit(solution)/shard_map/all_to_all | solution.py:179
  932.9 6.0 copy-start.1
  932.9 159.5 %all-to-all-start.3 = ((bf16[16,2,256,128]{3,2,1,0:T(8,128)(2,1)}), bf16[16,2,256,128]{3,2,1,0:T(8,128)(2,1)}, u32[]{:S(2)}, u32[]{:S(2)}) async-start(bf16[16,2,256,128]{3,2,1,0:T(8,128)(2,1)} %shard_map.58), calls=%async_computation.3 | async-start | bytes 4194304 | tf_op jit(solution)/shard_map/all_to_all | solution.py:179
where the time goes:
time: 1340 us
  Pallas kernels  1110 us (83%)
  blocking collectives  178 us (13%)
  starting transfers between devices  50.9 us (4%)
    pallas_call x3, Pallas kernels, on_device(): pl.pallas_call(functools.partial(pack_kernel, slots, reqs), out_shape=jax...  580 us
    pallas_call x3, Pallas kernels, on_device(): pl.pallas_call(functools.partial(attend_kernel, window), out_shape=jax.Sh...  333 us
    pallas_call x1, Pallas kernels, on_device(): pl.pallas_call(functools.partial(unpack_kernel, chunks, reqs), out_shape=...  193 us
    all_gather x1, blocking collectives, on_device(): lists = lax.all_gather(tile_list, 'seq', axis=1, tiled=True).reshape(-1)  127 us
    all_to_all x1, blocking collectives, on_device(): lax.all_to_all(done, 'seq', split_axis=0, concat_axis=0, tiled=True)  51 us
    all_to_all x2, starting transfers between devices, on_device(): lax.all_to_all(done, 'seq', split_axis=0, concat_axis=0, tiled=True)  31.5 us
  transfers between devices with their start and end apart: 5, of which 0 were waited for; matrix products, arithmetic and copies ran while one was open for 0% of the time, Pallas kernels for 54%

commit v1 on v0

v1 whole, which is shorter than its diff:
```python
import functools

import jax
import jax.numpy as jnp
from jax import lax
from jax.experimental import pallas as pl
from jax.experimental.pallas import tpu as pltpu
from jax.sharding import PartitionSpec as P

GROUP = 4
LOG2E = 1.4426950408889634


def pick(group, j, groups):
    return j * groups + (group if j % 2 == 0 else groups - 1 - group)


def pick_traced(group, j, groups):
    return j * groups + jnp.where(j % 2 == 0, group, groups - 1 - group)


def pack_kernel(order, queries, keys, values, before, out):
    out[:, 0, 0] = queries[...]
    out[:, 0, 1] = keys[...]
    out[:, 0, 2] = values[...]


def unpack_kernel(order, *refs):
    out = refs[-1]
    for chunk, array in enumerate(refs[:-1]):

        @pl.when(pl.program_id(0) == chunk)
        def store():
            out[...] = array[:, 0]


def attend_kernel(window, owned, counts, lists, data, before, out, turned, columns):
    tiles = data.shape[0]
    rows, width = data.shape[3:]
    head = owned[pl.program_id(0)]
    count = counts[head]
    group = GROUP if tiles % GROUP == 0 else 1
    factor = width ** (-0.5) * LOG2E

    @pl.loop(0, tiles)
    def turn(tile):
        turned[tile, :width, :] = data[tile, 0, 2].T
        turned[tile, width:, :] = jnp.ones((16, rows), jnp.bfloat16)
        columns[tile] = data[tile, 0, 0].T

    @pl.loop(0, tiles // group)
    def some_tiles(block):
        first = block * group
        bases = [(head * tiles + first + g) * window for g in range(group)]

        def advance(slot, carry):
            result = []
            for g in range(group):
                running, accum = carry[g]
                picked = lists[bases[g] + slot]
                scores = jnp.dot(
                    data[picked, 0, 1], columns[first + g], preferred_element_type=jnp.float32
                )
                newmax = jnp.maximum(running, jnp.max(scores, axis=0, keepdims=True) * factor)
                carried = jnp.exp2(running - newmax)
                weights = jnp.exp2(scores * factor - newmax).astype(jnp.bfloat16)
                accum = carried * accum + jnp.dot(
                    turned[picked], weights, preferred_element_type=jnp.float32
                )
                result.append((newmax, accum))
            return tuple(result)

        start = tuple(
            (
                jnp.full((1, rows), -1e30, jnp.float32),
                jnp.zeros((width + 16, rows), jnp.float32),
            )
            for _ in range(group)
        )
        done = lax.fori_loop(0, count, advance, start)
        for g in range(group):
            accum = done[g][1]
            ratio = accum[:width] / accum[width : width + 1]
            out[first + g, 0] = ratio.T.astype(jnp.bfloat16)


def on_device(queries, keys, values, tile_list, head_counts):
    reqs, rows, model_width = queries.shape
    heads = head_counts.shape[0]
    window = tile_list.shape[2]
    width = model_width // heads
    devices = lax.axis_size("seq")
    tasks = reqs * heads
    per_device = tasks // devices
    groups = devices // reqs
    me = lax.axis_index("seq")
    each = 1
    starts = range(0, per_device, each)

    ids = jnp.arange(heads, dtype=jnp.int32)
    mine, other = head_counts[:, None], head_counts[None, :]
    ahead = (other > mine) | ((other == mine) & (ids[None, :] < ids[:, None]))
    ranks = jnp.sum(ahead.astype(jnp.int32), axis=1)
    order = jnp.sum(jnp.where(ranks[None, :] == ids[:, None], ids[None, :], 0), axis=1)

    lists = lax.all_gather(tile_list, "seq", axis=1, tiled=True).reshape(-1)
    order, lists = lax.optimization_barrier((order, lists))

    hbm = pl.BlockSpec(memory_space=pl.ANY)

    def from_head(begin):
        def index(g, i, order):
            return (0, 0, order[pick_traced(g, begin + i, groups)])

        return pl.BlockSpec((reqs, rows, width), index)

    def send(begin, before):
        packed = pl.pallas_call(
            pack_kernel,
            out_shape=jax.ShapeDtypeStruct((devices, each, 3, rows, width), jnp.bfloat16),
            grid_spec=pltpu.PrefetchScalarGridSpec(
                num_scalar_prefetch=1,
                grid=(groups, each),
                in_specs=[from_head(begin)] * 3 + [hbm],
                out_specs=pl.BlockSpec(
                    (reqs, 1, 3, rows, width), lambda g, i, *_: (g, i, 0, 0, 0)
                ),
            ),
        )(order, queries, keys, values, before)
        return packed, lax.all_to_all(packed, "seq", split_axis=0, concat_axis=0, tiled=True)

    returned = []
    done = order
    packed, following = send(0, order)
    for begin in starts:
        data = following
        if begin + 1 < per_device:
            packed, following = send(begin + 1, done if begin else packed)
        spots = jnp.stack([pick(me // reqs, begin + i, groups) for i in range(each)])
        owned = jnp.sum(jnp.where(spots[:, None] == ids[None, :], order[None, :], 0), axis=1)
        done = pl.pallas_call(
            functools.partial(attend_kernel, window),
            out_shape=jax.ShapeDtypeStruct((devices, each, rows, width), jnp.bfloat16),
            grid_spec=pltpu.PrefetchScalarGridSpec(
                num_scalar_prefetch=3,
                grid=(each,),
                in_specs=[
                    pl.BlockSpec((devices, 1, 3, rows, width), lambda i, *_: (0, i, 0, 0, 0)),
                    hbm,
                ],
                out_specs=pl.BlockSpec((devices, 1, rows, width), lambda i, *_: (0, i, 0, 0)),
                scratch_shapes=[
                    pltpu.VMEM((devices, width + 16, rows), jnp.bfloat16),
                    pltpu.VMEM((devices, width, rows), jnp.bfloat16),
                ],
            ),
            compiler_params=pltpu.CompilerParams(vmem_limit_bytes=40 * 1024 * 1024),
            cost_estimate=pl.CostEstimate(
                flops=each * devices * 20 * 4 * rows * rows * width,
                bytes_accessed=each * devices * 4 * rows * width * 2,
                transcendentals=each * devices * 10 * rows * rows,
            ),
        )(owned, head_counts, lists, data, done)
        returned.append(lax.all_to_all(done, "seq", split_axis=0, concat_axis=0, tiled=True))

    def from_chunk(chunk):
        def index(c, i, g, order):
            now = c == chunk
            last = c > chunk
            hold = jnp.where(last, groups - 1, 0)
            return (jnp.where(now, g, hold), jnp.where(now, i, jnp.where(last, each - 1, 0)), 0, 0)

        return pl.BlockSpec((reqs, 1, rows, width), index)

    return pl.pallas_call(
        unpack_kernel,
        out_shape=jax.ShapeDtypeStruct(queries.shape, jnp.bfloat16),
        grid_spec=pltpu.PrefetchScalarGridSpec(
            num_scalar_prefetch=1,
            grid=(len(starts), each, groups),
            in_specs=[from_chunk(chunk) for chunk in range(len(starts))],
            out_specs=pl.BlockSpec(
                (reqs, rows, width),
                lambda c, i, g, order: (0, 0, order[pick_traced(g, c * each + i, groups)]),
            ),
        ),
    )(order, *returned)


def solution(mesh):
    in_specs = (
        P("groups", "seq", None),
        P("groups", "seq", None),
        P("groups", "seq", None),
        P(None, "seq", None),
        P(),
    )
    out_specs = P("groups", "seq", None)
    return jax.shard_map(
        on_device, mesh=mesh, in_specs=in_specs, out_specs=out_specs, check_vma=False
    )
```

time: 1340 us -> 922 us (0.69); the launches traced: 1340 us -> 905 us
  Pallas kernels: 1110 us -> 386 us
  waiting for transfers between devices: 0.01 us -> 201 us
  blocking collectives: 178 us -> 254 us
    pallas_call x4 -> x7, Pallas kernels: 773 us -> 45.2 us  [the longest x6 29.3 us: send(): pl.pallas_call(pack_kernel, out_shape=jax.ShapeDtypeStruct((devices, each...]
    all_to_all x0 -> x2, blocking collectives: none -> 171 us  [send(): lax.all_to_all(packed, 'seq', split_axis=0, concat_axis=0, tiled=True)]
    all_to_all x3 -> x4, waiting for transfers between devices: 0.01 us -> 164 us  [send(): lax.all_to_all(packed, 'seq', split_axis=0, concat_axis=0, tiled=True)]
    all_gather x1, blocking collectives: 127 us -> 23.6 us  [on_device(): lists = lax.all_gather(tile_list, 'seq', axis=1, tiled=True).reshape(-1)]
    all_to_all x2 -> x4, waiting for transfers between devices: 0.01 us -> 36.6 us  [on_device(): lax.all_to_all(done, 'seq', split_axis=0, concat_axis=0, tiled=True)]
    all_to_all x3 -> x4, starting transfers between devices: 19.4 us -> 32.1 us  [send(): lax.all_to_all(packed, 'seq', split_axis=0, concat_axis=0, tiled=True)]
    all_to_all x1 -> x2, blocking collectives: 51 us -> 60.2 us  [on_device(): lax.all_to_all(done, 'seq', split_axis=0, concat_axis=0, tiled=True)]
    pallas_call x3 -> x6, Pallas kernels: 333 us -> 341 us  [on_device(): pl.pallas_call(functools.partial(attend_kernel, window), out_shape=jax.Sh...]
  transfers between devices with their start and end apart: 5 -> 8, of which waited for: 0 -> 5; matrix products, arithmetic and copies ran while one was open for 0% -> 0% of each run, Pallas kernels for 54% -> 33%
where the time goes in v1:
time: 922 us; the launch traced here: 905 us
  Pallas kernels  386 us (42%)
  blocking collectives  254 us (28%)
  waiting for transfers between devices  201 us (22%)
  starting transfers between devices  57.6 us (6%)
    pallas_call x6, Pallas kernels, on_device(): pl.pallas_call(functools.partial(attend_kernel, window), out_shape=jax.Sh...  341 us
    all_to_all x2, blocking collectives, send(): lax.all_to_all(packed, 'seq', split_axis=0, concat_axis=0, tiled=True)  171 us
    all_to_all x4, waiting for transfers between devices, send(): lax.all_to_all(packed, 'seq', split_axis=0, concat_axis=0, tiled=True)  164 us
    all_to_all x2, blocking collectives, on_device(): lax.all_to_all(done, 'seq', split_axis=0, concat_axis=0, tiled=True)  60.2 us
    all_to_all x4, waiting for transfers between devices, on_device(): lax.all_to_all(done, 'seq', split_axis=0, concat_axis=0, tiled=True)  36.6 us
    all_to_all x4, starting transfers between devices, send(): lax.all_to_all(packed, 'seq', split_axis=0, concat_axis=0, tiled=True)  32.1 us
    pallas_call x6, Pallas kernels, send(): pl.pallas_call(pack_kernel, out_shape=jax.ShapeDtypeStruct((devices, each...  29.3 us
    all_to_all x4, starting transfers between devices, on_device(): lax.all_to_all(done, 'seq', split_axis=0, concat_axis=0, tiled=True)  25.5 us
  transfers between devices with their start and end apart: 8, of which 5 were waited for; matrix products, arithmetic and copies ran while one was open for 0% of the time, Pallas kernels for 33%

profile of v1, /device:TPU:1, one launch (start us, length us, event | category | flops | bytes accessed | tf_op | source)
XLA Modules:
  0.0 904.7 jit_solution(661322204547163244)
XLA Ops:
  0.0 23.6 %all_gather.3 = s32[24,16,16]{0,2,1:T(8,128)S(1)} all-gather(s32[24,1,16]{0,2,1:T(8,128)} %param.8), channel_id=1, replica_groups=mesh['groups'=2,'seq'=16] {'seq'}, dimensions={1}, use_global_device_ids=true | all-gather | bytes 26112 | tf_op jit(solution)/shard_map/all_gather | solution.py:106
  23.6 0.1 copy.8
  23.7 0.1 reshape.48.lists
  23.8 0.9 convert_reduce_fusion
  24.7 0.7 select_reduce_fusion.order.before
  25.4 4.9 shard_map.55.before
  30.3 3.7 all-to-all-start
  34.0 4.9 shard_map.57
  38.9 0.0 copy-start.3
  38.9 0.0 copy-start.4
  38.9 54.9 %all-to-all-done.data = bf16[16,1,3,256,128]{4,3,2,1,0:T(8,128)(2,1)S(1)} async-done(((bf16[16,1,3,256,128]{4,3,2,1,0:T(8,128)(2,1)}), bf16[16,1,3,256,128]{4,3,2,1,0:T(8,128)(2,1)S(1)}, u32[]{:S(2)}, u32[]{:S(2)}) %all-to-all-start) | async-done | bytes 3145760 | tf_op jit(solution)/shard_map/all_to_all | solution.py:130
  93.8 15.1 %all-to-all-start.2 = ((bf16[16,1,3,256,128]{4,3,2,1,0:T(8,128)(2,1)}), bf16[16,1,3,256,128]{4,3,2,1,0:T(8,128)(2,1)}, u32[]{:S(2)}, u32[]{:S(2)}) async-start(bf16[16,1,3,256,128]{4,3,2,1,0:T(8,128)(2,1)} %shard_map.57), calls=%async_computation.2 | async-start | bytes 6291456 | tf_op jit(solution)/shard_map/all_to_all | solution.py:130
  108.8 0.0 copy-done.3
  108.8 0.7 fusion.7
  109.6 0.0 copy-done.4
  109.6 93.9 %shard_map.56.before = bf16[16,1,256,128]{3,2,1,0:T(8,128)(2,1)} custom-call(s32[1]{0:T(128)} %bitcast.owned, s32[24]{0:T(128)S(1)} %copy-done.4, s32[6144]{0:T(1024)S(1)} %reshape.48.lists, bf16[16,1,3,256,128]{4,3,2,1,0:T(8,128)(2,1)S(1)} %all-to-all-done.data, s32[24]{0:T(128)S(1)} %copy-done.3), custom_call_target="tpu_custom_call" | custom-call | flops 10737418240 | bytes 4194304 | tf_op jit(solution)/shard_map/pallas_call | solution.py:141
  203.4 0.0 all-to-all-done.2.data
  203.4 67.8 %shard_map.58.before = bf16[16,1,256,128]{3,2,1,0:T(8,128)(2,1)} custom-call(s32[1]{0:T(128)} %bitcast.1.owned, s32[24]{0:T(128)S(1)} %copy-done.4, s32[6144]{0:T(1024)S(1)} %reshape.48.lists, bf16[16,1,3,256,128]{4,3,2,1,0:T(8,128)(2,1)} %all-to-all-done.2.data, bf16[16,1,256,128]{3,2,1,0:T(8,128)(2,1)} %shard_map.56.before), custom_call_target="tpu_custom_call" | custom-call | flops 10737418240 | bytes 4194304 | tf_op jit(solution)/shard_map/pallas_call | solution.py:141
  271.3 6.0 all-to-all-start.3
  277.3 4.9 shard_map.59
  282.1 18.3 %all-to-all-done.3.refs_1_ = bf16[16,1,256,128]{3,2,1,0:T(8,128)(2,1)S(1)} async-done(((bf16[16,1,256,128]{3,2,1,0:T(8,128)(2,1)}), bf16[16,1,256,128]{3,2,1,0:T(8,128)(2,1)S(1)}, u32[]{:S(2)}, u32[]{:S(2)}) %all-to-all-start.3) | async-done | bytes 1048608 | tf_op jit(solution)/shard_map/all_to_all | solution.py:164
  300.4 0.0 copy-start.5
  300.4 1.0 copy-done.5
  301.4 6.7 all-to-all-start.4
  308.1 4.9 shard_map.61
  313.0 54.8 %all-to-all-done.4.data = bf16[16,1,3,256,128]{4,3,2,1,0:T(8,128)(2,1)S(1)} async-done(((bf16[16,1,3,256,128]{4,3,2,1,0:T(8,128)(2,1)}), bf16[16,1,3,256,128]{4,3,2,1,0:T(8,128)(2,1)S(1)}, u32[]{:S(2)}, u32[]{:S(2)}) %all-to-all-start.4) | async-done | bytes 3145760 | tf_op jit(solution)/shard_map/all_to_all | solution.py:130
  367.8 85.3 %all_to_all.60.data = bf16[16,1,3,256,128]{4,3,2,1,0:T(8,128)(2,1)} all-to-all(bf16[16,1,3,256,128]{4,3,2,1,0:T(8,128)(2,1)} %shard_map.61), channel_id=1, replica_groups=mesh['groups'=2,'seq'=16] {'seq'}, dimensions={0} | all-to-all | bytes 6291456 | tf_op jit(solution)/shard_map/all_to_all | solution.py:130
  453.1 4.8 all-to-all-start.1
  458.0 0.0 copy-start.1
  458.0 66.1 %shard_map.60.before = bf16[16,1,256,128]{3,2,1,0:T(8,128)(2,1)} custom-call(s32[1]{0:T(128)} %bitcast.2.owned, s32[24]{0:T(128)S(1)} %copy-done.4, s32[6144]{0:T(1024)S(1)} %reshape.48.lists, bf16[16,1,3,256,128]{4,3,2,1,0:T(8,128)(2,1)S(1)} %all-to-all-done.4.data, bf16[16,1,256,128]{3,2,1,0:T(8,128)(2,1)} %shard_map.58.before), custom_call_target="tpu_custom_call" | custom-call | flops 10737418240 | bytes 4194304 | tf_op jit(solution)/shard_map/pallas_call | solution.py:141
  524.1 0.0 copy-done.1
  524.1 43.8 %shard_map.62.before = bf16[16,1,256,128]{3,2,1,0:T(8,128)(2,1)} custom-call(s32[1]{0:T(128)} %bitcast.3.owned, s32[24]{0:T(128)S(1)} %copy-done.4, s32[6144]{0:T(1024)S(1)} %reshape.48.lists, bf16[16,1,3,256,128]{4,3,2,1,0:T(8,128)(2,1)S(1)} %copy-done.1, bf16[16,1,256,128]{3,2,1,0:T(8,128)(2,1)} %shard_map.60.before), custom_call_target="tpu_custom_call" | custom-call | flops 10737418240 | bytes 4194304 | tf_op jit(solution)/shard_map/pallas_call | solution.py:141
  567.9 0.0 all-to-all-done.1.refs_0_
  567.9 9.8 %all-to-all-start.7 = ((bf16[16,1,256,128]{3,2,1,0:T(8,128)(2,1)}), bf16[16,1,256,128]{3,2,1,0:T(8,128)(2,1)S(1)}, u32[]{:S(2)}, u32[]{:S(2)}) async-start(bf16[16,1,256,128]{3,2,1,0:T(8,128)(2,1)} %shard_map.62.before), calls=%async_computation.7 | async-start | bytes 2097152 | tf_op jit(solution)/shard_map/all_to_all | solution.py:164
  577.6 4.9 shard_map.63
  582.5 18.3 %all-to-all-done.7.refs_3_ = bf16[16,1,256,128]{3,2,1,0:T(8,128)(2,1)S(1)} async-done(((bf16[16,1,256,128]{3,2,1,0:T(8,128)(2,1)}), bf16[16,1,256,128]{3,2,1,0:T(8,128)(2,1)S(1)}, u32[]{:S(2)}, u32[]{:S(2)}) %all-to-all-start.7) | async-done | bytes 1048608 | tf_op jit(solution)/shard_map/all_to_all | solution.py:164
  600.8 0.0 copy-start.6
  600.8 1.1 copy-done.6
  601.8 6.7 all-to-all-start.8
  608.5 4.9 shard_map.65
  613.4 54.8 %all-to-all-done.8.data = bf16[16,1,3,256,128]{4,3,2,1,0:T(8,128)(2,1)S(1)} async-done(((bf16[16,1,3,256,128]{4,3,2,1,0:T(8,128)(2,1)}), bf16[16,1,3,256,128]{4,3,2,1,0:T(8,128)(2,1)S(1)}, u32[]{:S(2)}, u32[]{:S(2)}) %all-to-all-start.8) | async-done | bytes 3145760 | tf_op jit(solution)/shard_map/all_to_all | solution.py:130
  668.2 85.3 %all_to_all.61.data = bf16[16,1,3,256,128]{4,3,2,1,0:T(8,128)(2,1)} all-to-all(bf16[16,1,3,256,128]{4,3,2,1,0:T(8,128)(2,1)} %shard_map.65), channel_id=1, replica_groups=mesh['groups'=2,'seq'=16] {'seq'}, dimensions={0} | all-to-all | bytes 6291456 | tf_op jit(solution)/shard_map/all_to_all | solution.py:130
  753.6 4.8 all-to-all-start.5
  758.4 0.0 copy-start
  758.4 43.0 %shard_map.64.before = bf16[16,1,256,128]{3,2,1,0:T(8,128)(2,1)S(1)} custom-call(s32[1]{0:T(128)} %bitcast.4.owned, s32[24]{0:T(128)S(1)} %copy-done.4, s32[6144]{0:T(1024)S(1)} %reshape.48.lists, bf16[16,1,3,256,128]{4,3,2,1,0:T(8,128)(2,1)S(1)} %all-to-all-done.8.data, bf16[16,1,256,128]{3,2,1,0:T(8,128)(2,1)} %shard_map.62.before), custom_call_target="tpu_custom_call" | custom-call | flops 10737418240 | bytes 4194304 | tf_op jit(solution)/shard_map/pallas_call | solution.py:141
  801.4 0.0 copy-done
  801.4 26.2 %shard_map.66 = bf16[16,1,256,128]{3,2,1,0:T(8,128)(2,1)S(1)} custom-call(s32[1]{0:T(128)} %bitcast.5.owned, s32[24]{0:T(128)S(1)} %copy-done.4, s32[6144]{0:T(1024)S(1)} %reshape.48.lists, bf16[16,1,3,256,128]{4,3,2,1,0:T(8,128)(2,1)S(1)} %copy-done, bf16[16,1,256,128]{3,2,1,0:T(8,128)(2,1)S(1)} %shard_map.64.before), custom_call_target="tpu_custom_call" | custom-call | flops 10737418240 | bytes 4194304 | tf_op jit(solution)/shard_map/pallas_call | solution.py:141
  827.6 0.0 copy-start.2
  827.6 1.0 copy-done.2
  828.6 0.0 all-to-all-done.5.refs_2_
  828.6 30.2 %all_to_all.62.refs_5_ = bf16[16,1,256,128]{3,2,1,0:T(8,128)(2,1)} all-to-all(bf16[16,1,256,128]{3,2,1,0:T(8,128)(2,1)S(1)} %shard_map.66), channel_id=1, replica_groups=mesh['groups'=2,'seq'=16] {'seq'}, dimensions={0} | all-to-all | bytes 2097152 | tf_op jit(solution)/shard_map/all_to_all | solution.py:164
  858.8 29.9 %all_to_all.63.refs_4_ = bf16[16,1,256,128]{3,2,1,0:T(8,128)(2,1)} all-to-all(bf16[16,1,256,128]{3,2,1,0:T(8,128)(2,1)} %copy-done.2), channel_id=1, replica_groups=mesh['groups'=2,'seq'=16] {'seq'}, dimensions={0} | all-to-all | bytes 2097152 | tf_op jit(solution)/shard_map/all_to_all | solution.py:164
  888.7 15.9 %shard_map.67 = bf16[4,256,3072]{2,1,0:T(8,128)(2,1)} custom-call(s32[24]{0:T(128)} %select_reduce_fusion.order.before, bf16[16,1,256,128]{3,2,1,0:T(8,128)(2,1)} %all-to-all-done.1.refs_0_, bf16[16,1,256,128]{3,2,1,0:T(8,128)(2,1)} %copy-done.5, bf16[16,1,256,128]{3,2,1,0:T(8,128)(2,1)} %all-to-all-done.5.refs_2_, bf16[16,1,256,128]{3,2,1,0:T(8,128)(2,1)} %copy-done.6, ...), custom_call_target="tpu_custom_call" | custom-call | tf_op jit(solution)/shard_map/pallas_call | solution.py:175
Async XLA Ops:
  30.3 63.5 %all-to-all-start = ((bf16[16,1,3,256,128]{4,3,2,1,0:T(8,128)(2,1)}), bf16[16,1,3,256,128]{4,3,2,1,0:T(8,128)(2,1)S(1)}, u32[]{:S(2)}, u32[]{:S(2)}) async-start(bf16[16,1,3,256,128]{4,3,2,1,0:T(8,128)(2,1)} %shard_map.55.before), calls=%async_computation | async-start | bytes 6291456 | tf_op jit(solution)/shard_map/all_to_all | solution.py:130
  38.9 69.9 %copy-start.3 = (s32[24]{0:T(128)S(1)}, s32[24]{0:T(128)}, u32[]{:S(2)}) copy-start(s32[24]{0:T(128)} %select_reduce_fusion.order.before) | copy-start | bytes 292
  38.9 70.7 %copy-start.4 = (s32[24]{0:T(128)S(1)}, s32[24]{0:T(128)}, u32[]{:S(2)}) copy-start(s32[24]{0:T(128)} %counts.11) | copy-start | bytes 292
  93.8 109.7 %all-to-all-start.2 = ((bf16[16,1,3,256,128]{4,3,2,1,0:T(8,128)(2,1)}), bf16[16,1,3,256,128]{4,3,2,1,0:T(8,128)(2,1)}, u32[]{:S(2)}, u32[]{:S(2)}) async-start(bf16[16,1,3,256,128]{4,3,2,1,0:T(8,128)(2,1)} %shard_map.57), calls=%async_computation.2 | async-start | bytes 6291456 | tf_op jit(solution)/shard_map/all_to_all | solution.py:130
  271.3 29.1 %all-to-all-start.3 = ((bf16[16,1,256,128]{3,2,1,0:T(8,128)(2,1)}), bf16[16,1,256,128]{3,2,1,0:T(8,128)(2,1)S(1)}, u32[]{:S(2)}, u32[]{:S(2)}) async-start(bf16[16,1,256,128]{3,2,1,0:T(8,128)(2,1)} %shard_map.58.before), calls=%async_computation.3 | async-start | bytes 2097152 | tf_op jit(solution)/shard_map/all_to_all | solution.py:164
  300.4 1.0 copy-start.5
  301.4 66.4 %all-to-all-start.4 = ((bf16[16,1,3,256,128]{4,3,2,1,0:T(8,128)(2,1)}), bf16[16,1,3,256,128]{4,3,2,1,0:T(8,128)(2,1)S(1)}, u32[]{:S(2)}, u32[]{:S(2)}) async-start(bf16[16,1,3,256,128]{4,3,2,1,0:T(8,128)(2,1)} %shard_map.59), calls=%async_computation.4 | async-start | bytes 6291456 | tf_op jit(solution)/shard_map/all_to_all | solution.py:130
  453.1 114.7 %all-to-all-start.1 = ((bf16[16,1,256,128]{3,2,1,0:T(8,128)(2,1)}), bf16[16,1,256,128]{3,2,1,0:T(8,128)(2,1)}, u32[]{:S(2)}, u32[]{:S(2)}) async-start(bf16[16,1,256,128]{3,2,1,0:T(8,128)(2,1)} %shard_map.56.before), calls=%async_computation.1 | async-start | bytes 2097152 | tf_op jit(solution)/shard_map/all_to_all | solution.py:164
  458.0 66.1 %copy-start.1 = (bf16[16,1,3,256,128]{4,3,2,1,0:T(8,128)(2,1)S(1)}, bf16[16,1,3,256,128]{4,3,2,1,0:T(8,128)(2,1)}, u32[]{:S(2)}) copy-start(bf16[16,1,3,256,128]{4,3,2,1,0:T(8,128)(2,1)} %all_to_all.60.data) | copy-start | bytes 9437188
  567.9 32.9 %all-to-all-start.7 = ((bf16[16,1,256,128]{3,2,1,0:T(8,128)(2,1)}), bf16[16,1,256,128]{3,2,1,0:T(8,128)(2,1)S(1)}, u32[]{:S(2)}, u32[]{:S(2)}) async-start(bf16[16,1,256,128]{3,2,1,0:T(8,128)(2,1)} %shard_map.62.before), calls=%async_computation.7 | async-start | bytes 2097152 | tf_op jit(solution)/shard_map/all_to_all | solution.py:164
  600.8 1.1 copy-start.6
  601.8 66.4 %all-to-all-start.8 = ((bf16[16,1,3,256,128]{4,3,2,1,0:T(8,128)(2,1)}), bf16[16,1,3,256,128]{4,3,2,1,0:T(8,128)(2,1)S(1)}, u32[]{:S(2)}, u32[]{:S(2)}) async-start(bf16[16,1,3,256,128]{4,3,2,1,0:T(8,128)(2,1)} %shard_map.63), calls=%async_computation.8 | async-start | bytes 6291456 | tf_op jit(solution)/shard_map/all_to_all | solution.py:130
  753.6 75.0 %all-to-all-start.5 = ((bf16[16,1,256,128]{3,2,1,0:T(8,128)(2,1)}), bf16[16,1,256,128]{3,2,1,0:T(8,128)(2,1)}, u32[]{:S(2)}, u32[]{:S(2)}) async-start(bf16[16,1,256,128]{3,2,1,0:T(8,128)(2,1)} %shard_map.60.before), calls=%async_computation.5 | async-start | bytes 2097152 | tf_op jit(solution)/shard_map/all_to_all | solution.py:164
  758.4 43.0 %copy-start = (bf16[16,1,3,256,128]{4,3,2,1,0:T(8,128)(2,1)S(1)}, bf16[16,1,3,256,128]{4,3,2,1,0:T(8,128)(2,1)}, u32[]{:S(2)}) copy-start(bf16[16,1,3,256,128]{4,3,2,1,0:T(8,128)(2,1)} %all_to_all.61.data) | copy-start | bytes 9437188
  827.6 1.0 copy-start.2

commit v2 on v1

--- a/solution.py
+++ b/solution.py
@@ -25,16 +25,21 @@
     out[:, 0, 2] = values[...]
 
 
-def unpack_kernel(order, *refs):
+def unpack_kernel(spans, order, *refs):
     out = refs[-1]
-    for chunk, array in enumerate(refs[:-1]):
-
-        @pl.when(pl.program_id(0) == chunk)
+    now = pl.program_id(0)
+    for (begin, end), array in zip(spans, refs[:-1]):
+
+        @pl.when((now >= begin) & (now < end))
         def store():
             out[...] = array[:, 0]
 
 
-def attend_kernel(window, owned, counts, lists, data, before, out, turned, columns):
+def at_task(task, i, *_):
+    return (0, task + i, 0, 0)
+
+
+def attend_kernel(window, owned, counts, lists, data, before, ahead, out, turned, columns):
     tiles = data.shape[0]
     rows, width = data.shape[3:]
     head = owned[pl.program_id(0)]
@@ -95,7 +100,8 @@
     groups = devices // reqs
     me = lax.axis_index("seq")
     each = 1
-    starts = range(0, per_device, each)
+    split = max(per_device - 1, 1)
+    spans = [(0, split), (split, per_device)] if split < per_device else [(0, split)]
 
     ids = jnp.arange(heads, dtype=jnp.int32)
     mine, other = head_counts[:, None], head_counts[None, :]
@@ -132,23 +138,28 @@
     returned = []
     done = order
     packed, following = send(0, order)
-    for begin in starts:
+    for step in range(per_device):
         data = following
-        if begin + 1 < per_device:
-            packed, following = send(begin + 1, done if begin else packed)
-        spots = jnp.stack([pick(me // reqs, begin + i, groups) for i in range(each)])
+        if step + 1 < per_device:
+            packed, following = send(step + 1, done if step else packed)
+        begin, end = spans[0] if step < split else spans[1]
+        spots = jnp.stack([pick(me // reqs, step + i, groups) for i in range(each)])
         owned = jnp.sum(jnp.where(spots[:, None] == ids[None, :], order[None, :], 0), axis=1)
         done = pl.pallas_call(
             functools.partial(attend_kernel, window),
-            out_shape=jax.ShapeDtypeStruct((devices, each, rows, width), jnp.bfloat16),
+            out_shape=jax.ShapeDtypeStruct((devices, end - begin, rows, width), jnp.bfloat16),
+            input_output_aliases={} if step == begin else {4: 0},
             grid_spec=pltpu.PrefetchScalarGridSpec(
                 num_scalar_prefetch=3,
                 grid=(each,),
                 in_specs=[
                     pl.BlockSpec((devices, 1, 3, rows, width), lambda i, *_: (0, i, 0, 0, 0)),
                     hbm,
+                    hbm,
                 ],
-                out_specs=pl.BlockSpec((devices, 1, rows, width), lambda i, *_: (0, i, 0, 0)),
+                out_specs=pl.BlockSpec(
+                    (devices, 1, rows, width), functools.partial(at_task, step - begin)
+                ),
                 scratch_shapes=[
                     pltpu.VMEM((devices, width + 16, rows), jnp.bfloat16),
                     pltpu.VMEM((devices, width, rows), jnp.bfloat16),
@@ -160,28 +171,30 @@
                 bytes_accessed=each * devices * 4 * rows * width * 2,
                 transcendentals=each * devices * 10 * rows * rows,
             ),
-        )(owned, head_counts, lists, data, done)
-        returned.append(lax.all_to_all(done, "seq", split_axis=0, concat_axis=0, tiled=True))
-
-    def from_chunk(chunk):
-        def index(c, i, g, order):
-            now = c == chunk
-            last = c > chunk
-            hold = jnp.where(last, groups - 1, 0)
-            return (jnp.where(now, g, hold), jnp.where(now, i, jnp.where(last, each - 1, 0)), 0, 0)
+        )(owned, head_counts, lists, data, done, packed)
+        if step + 1 == end:
+            returned.append(
+                lax.all_to_all(done, "seq", split_axis=0, concat_axis=0, tiled=True)
+            )
+
+    def from_span(begin, end):
+        def index(j, g, order):
+            before, after = j < begin, j >= end
+            row = jnp.where(before, 0, jnp.where(after, groups - 1, g))
+            return (row, jnp.clip(j - begin, 0, end - begin - 1), 0, 0)
 
         return pl.BlockSpec((reqs, 1, rows, width), index)
 
     return pl.pallas_call(
-        unpack_kernel,
+        functools.partial(unpack_kernel, spans),
         out_shape=jax.ShapeDtypeStruct(queries.shape, jnp.bfloat16),
         grid_spec=pltpu.PrefetchScalarGridSpec(
             num_scalar_prefetch=1,
-            grid=(len(starts), each, groups),
-            in_specs=[from_chunk(chunk) for chunk in range(len(starts))],
+            grid=(per_device, groups),
+            in_specs=[from_span(begin, end) for begin, end in spans],
             out_specs=pl.BlockSpec(
                 (reqs, rows, width),
-                lambda c, i, g, order: (0, 0, order[pick_traced(g, c * each + i, groups)]),
+                lambda j, g, order: (0, 0, order[pick_traced(g, j, groups)]),
             ),
         ),
     )(order, *returned)

time: 922 us -> 739 us (0.80); the launches traced: 905 us -> 739 us
  waiting for transfers between devices: 201 us -> 59.7 us
  blocking collectives: 254 us -> 194 us
  Pallas kernels: 386 us -> 408 us
  local copies, waits for them, and re-layouts: 3.29 us -> 24.5 us
    all_to_all x2 -> x0, blocking collectives: 171 us -> none  [send(): lax.all_to_all(packed, 'seq', split_axis=0, concat_axis=0, tiled=True)]
    all_to_all x2, blocking collectives: 60.2 us -> 171 us  [on_device(): lax.all_to_all(done, 'seq', split_axis=0, concat_axis=0, tiled=True)]
    all_to_all x4 -> x6, waiting for transfers between devices: 164 us -> 59.7 us  [send(): lax.all_to_all(packed, 'seq', split_axis=0, concat_axis=0, tiled=True)]
    all_to_all x4 -> x0, waiting for transfers between devices: 36.6 us -> none  [on_device(): lax.all_to_all(done, 'seq', split_axis=0, concat_axis=0, tiled=True)]
    all_to_all x4 -> x0, starting transfers between devices: 25.5 us -> none  [on_device(): lax.all_to_all(done, 'seq', split_axis=0, concat_axis=0, tiled=True)]
    pallas_call x6, Pallas kernels: 341 us -> 363 us  [on_device(): pl.pallas_call(functools.partial(attend_kernel, window), out_shape=jax.Sh...]
    unnamed x14 -> x34, local copies, waits for them, and re-layouts: 3.05 us -> 24.2 us
    all_to_all x4 -> x6, starting transfers between devices: 32.1 us -> 49.9 us  [send(): lax.all_to_all(packed, 'seq', split_axis=0, concat_axis=0, tiled=True)]
  transfers between devices with their start and end apart: 8 -> 6, of which waited for: 5 -> 2; matrix products, arithmetic and copies ran while one was open for 0% -> 0% of each run, Pallas kernels for 33% -> 49%
where the time goes in v2:
time: 739 us
  Pallas kernels  408 us (55%)
  blocking collectives  194 us (26%)
  waiting for transfers between devices  59.7 us (8%)
  starting transfers between devices  49.9 us (7%)
  local copies, waits for them, and re-layouts  24.5 us (3%)
    pallas_call x6, Pallas kernels, on_device(): pl.pallas_call(functools.partial(attend_kernel, window), out_shape=jax.Sh...  363 us
    all_to_all x2, blocking collectives, on_device(): lax.all_to_all(done, 'seq', split_axis=0, concat_axis=0, tiled=True)  171 us
    all_to_all x6, waiting for transfers between devices, send(): lax.all_to_all(packed, 'seq', split_axis=0, concat_axis=0, tiled=True)  59.7 us
    all_to_all x6, starting transfers between devices, send(): lax.all_to_all(packed, 'seq', split_axis=0, concat_axis=0, tiled=True)  49.9 us
    pallas_call x6, Pallas kernels, send(): pl.pallas_call(pack_kernel, out_shape=jax.ShapeDtypeStruct((devices, each...  29.4 us
    unnamed x34, local copies, waits for them, and re-layouts  24.2 us
    all_gather x1, blocking collectives, on_device(): lists = lax.all_gather(tile_list, 'seq', axis=1, tiled=True).reshape(-1)  23.6 us
    pallas_call x1, Pallas kernels, on_device(): pl.pallas_call(functools.partial(unpack_kernel, spans), out_shape=jax.Sha...  15.6 us
  transfers between devices with their start and end apart: 6, of which 2 were waited for; matrix products, arithmetic and copies ran while one was open for 0% of the time, Pallas kernels for 49%

profile of v2, /device:TPU:1, one launch (start us, length us, event | category | flops | bytes accessed | tf_op | source)
XLA Modules:
  0.0 738.7 jit_solution(16045063779419377283)
XLA Ops:
  0.0 23.6 %all_gather.3 = s32[24,16,16]{0,2,1:T(8,128)S(1)} all-gather(s32[24,1,16]{0,2,1:T(8,128)} %param.8), channel_id=1, replica_groups=mesh['groups'=2,'seq'=16] {'seq'}, dimensions={1}, use_global_device_ids=true | all-gather | bytes 26112 | tf_op jit(solution)/shard_map/all_gather | solution.py:112
  23.6 0.1 copy.12
  23.7 0.1 reshape.48.lists
  23.8 0.9 convert_reduce_fusion
  24.7 0.7 select_reduce_fusion.order.before
  25.4 4.9 shard_map.55.before
  30.3 4.4 all-to-all-start
  34.7 4.9 shard_map.56.ahead
  39.6 0.0 copy-start.15
  39.6 0.0 copy-start.14
  39.6 0.0 copy-start.16
  39.6 55.0 %all-to-all-done.data = bf16[16,1,3,256,128]{4,3,2,1,0:T(8,128)(2,1)} async-done(((bf16[16,1,3,256,128]{4,3,2,1,0:T(8,128)(2,1)}), bf16[16,1,3,256,128]{4,3,2,1,0:T(8,128)(2,1)}, u32[]{:S(2)}, u32[]{:S(2)}) %all-to-all-start) | async-done | bytes 3145760 | tf_op jit(solution)/shard_map/all_to_all | solution.py:136
  94.6 15.1 %all-to-all-start.2 = ((bf16[16,1,3,256,128]{4,3,2,1,0:T(8,128)(2,1)}), bf16[16,1,3,256,128]{4,3,2,1,0:T(8,128)(2,1)}, u32[]{:S(2)}, u32[]{:S(2)}) async-start(bf16[16,1,3,256,128]{4,3,2,1,0:T(8,128)(2,1)} %shard_map.56.ahead), calls=%async_computation.2 | async-start | bytes 6291456 | tf_op jit(solution)/shard_map/all_to_all | solution.py:136
  109.6 0.0 copy-done.15
  109.6 0.8 fusion.7
  110.4 0.0 copy-done.14
  110.4 0.0 copy-done.16
  110.4 94.7 %shard_map.57.before = bf16[16,5,256,128]{3,2,1,0:T(8,128)(2,1)S(1)} custom-call(s32[1]{0:T(128)} %bitcast.2.owned, s32[24]{0:T(128)S(1)} %copy-done.16, s32[6144]{0:T(1024)S(1)} %reshape.48.lists, bf16[16,1,3,256,128]{4,3,2,1,0:T(8,128)(2,1)} %all-to-all-done.data, s32[24]{0:T(128)S(1)} %copy-done.15, bf16[16,1,3,256,128]{4,3,2,1,0:T(8,128)(2,1)S(1)} %copy-done.14), custom_call_target="tpu_custom_call" | custom-call | flops 10737418240 | bytes 4194304 | tf_op jit(solution)/shard_map/pallas_call | solution.py:148
  205.1 0.0 copy-start
  205.1 2.3 copy-done
  207.4 5.0 shard_map.58.ahead
  212.4 0.0 copy-start.11
  212.4 0.0 all-to-all-done.2.data
  212.4 4.7 all-to-all-start.1
  217.0 0.0 copy-done.11
  217.0 0.0 copy-start.1
  217.1 2.5 copy-done.1
  219.5 72.5 %shard_map.59.before = bf16[16,5,256,128]{3,2,1,0:T(8,128)(2,1)S(1)} custom-call(s32[1]{0:T(128)} %bitcast.3.owned, s32[24]{0:T(128)S(1)} %copy-done.16, s32[6144]{0:T(1024)S(1)} %reshape.48.lists, bf16[16,1,3,256,128]{4,3,2,1,0:T(8,128)(2,1)} %all-to-all-done.2.data, bf16[16,5,256,128]{3,2,1,0:T(8,128)(2,1)S(1)} %copy-done.1, ...), custom_call_target="tpu_custom_call", output_to_operand_aliasing={{}: (4, {})} | custom-call | flops 10737418240 | bytes 4194304 | tf_op jit(solution)/shard_map/pallas_call | solution.py:148
  292.0 0.0 copy-start.2
  292.1 2.3 copy-done.2
  294.4 4.9 shard_map.60.ahead
  299.3 0.0 copy-start.12
  299.3 0.0 all-to-all-done.1.data
  299.3 6.4 all-to-all-start.4
  305.7 0.0 copy-done.12
  305.7 0.0 copy-start.3
  305.7 2.5 copy-done.3
  308.1 66.9 %shard_map.61.before = bf16[16,5,256,128]{3,2,1,0:T(8,128)(2,1)S(1)} custom-call(s32[1]{0:T(128)} %bitcast.1.owned, s32[24]{0:T(128)S(1)} %copy-done.16, s32[6144]{0:T(1024)S(1)} %reshape.48.lists, bf16[16,1,3,256,128]{4,3,2,1,0:T(8,128)(2,1)} %all-to-all-done.1.data, bf16[16,5,256,128]{3,2,1,0:T(8,128)(2,1)S(1)} %copy-done.3, ...), custom_call_target="tpu_custom_call", output_to_operand_aliasing={{}: (4, {})} | custom-call | flops 10737418240 | bytes 4194304 | tf_op jit(solution)/shard_map/pallas_call | solution.py:148
  375.0 0.0 copy-start.4
  375.0 2.3 copy-done.4
  377.4 4.9 shard_map.62.ahead
  382.2 0.0 all-to-all-done.4.data
  382.2 4.7 all-to-all-start.3
  386.9 0.0 copy-done.13
  386.9 0.0 copy-start.5
  386.9 2.5 copy-done.5
  389.4 50.3 %shard_map.63.before = bf16[16,5,256,128]{3,2,1,0:T(8,128)(2,1)S(1)} custom-call(s32[1]{0:T(128)} %bitcast.4.owned, s32[24]{0:T(128)S(1)} %copy-done.16, s32[6144]{0:T(1024)S(1)} %reshape.48.lists, bf16[16,1,3,256,128]{4,3,2,1,0:T(8,128)(2,1)} %all-to-all-done.4.data, bf16[16,5,256,128]{3,2,1,0:T(8,128)(2,1)S(1)} %copy-done.5, ...), custom_call_target="tpu_custom_call", output_to_operand_aliasing={{}: (4, {})} | custom-call | flops 10737418240 | bytes 4194304 | tf_op jit(solution)/shard_map/pallas_call | solution.py:148
  439.7 0.0 copy-start.6
  439.7 2.3 copy-done.6
  442.0 5.0 shard_map.64.ahead
  447.0 0.0 all-to-all-done.3.data
  447.0 14.8 %all-to-all-start.6 = ((bf16[16,1,3,256,128]{4,3,2,1,0:T(8,128)(2,1)}), bf16[16,1,3,256,128]{4,3,2,1,0:T(8,128)(2,1)}, u32[]{:S(2)}, u32[]{:S(2)}) async-start(bf16[16,1,3,256,128]{4,3,2,1,0:T(8,128)(2,1)} %shard_map.64.ahead), calls=%async_computation.6 | async-start | bytes 6291456 | tf_op jit(solution)/shard_map/all_to_all | solution.py:136
  461.8 0.0 copy-done.10
  461.8 0.0 copy-start.7
  461.8 2.5 copy-done.7
  464.3 50.3 %shard_map.65.before = bf16[16,5,256,128]{3,2,1,0:T(8,128)(2,1)S(1)} custom-call(s32[1]{0:T(128)} %bitcast.owned, s32[24]{0:T(128)S(1)} %copy-done.16, s32[6144]{0:T(1024)S(1)} %reshape.48.lists, bf16[16,1,3,256,128]{4,3,2,1,0:T(8,128)(2,1)} %all-to-all-done.3.data, bf16[16,5,256,128]{3,2,1,0:T(8,128)(2,1)S(1)} %copy-done.7, ...), custom_call_target="tpu_custom_call", output_to_operand_aliasing={{}: (4, {})} | custom-call | flops 10737418240 | bytes 4194304 | tf_op jit(solution)/shard_map/pallas_call | solution.py:148
  514.6 0.0 copy-start.8
  514.6 2.3 copy-done.8
  517.0 4.7 all-to-all-done.6.data
  521.6 2.5 copy-done.9
  524.1 28.1 %shard_map.66 = bf16[16,1,256,128]{3,2,1,0:T(8,128)(2,1)S(1)} custom-call(s32[1]{0:T(128)} %bitcast.5.owned, s32[24]{0:T(128)S(1)} %copy-done.16, s32[6144]{0:T(1024)S(1)} %reshape.48.lists, bf16[16,1,3,256,128]{4,3,2,1,0:T(8,128)(2,1)} %all-to-all-done.6.data, bf16[16,5,256,128]{3,2,1,0:T(8,128)(2,1)S(1)} %copy-done.9, ...), custom_call_target="tpu_custom_call" | custom-call | flops 10737418240 | bytes 4194304 | tf_op jit(solution)/shard_map/pallas_call | solution.py:148
  552.2 51.3 %all_to_all.40.refs_1_ = bf16[16,1,256,128]{3,2,1,0:T(8,128)(2,1)} all-to-all(bf16[16,1,256,128]{3,2,1,0:T(8,128)(2,1)S(1)} %shard_map.66), channel_id=1, replica_groups=mesh['groups'=2,'seq'=16] {'seq'}, dimensions={0} | all-to-all | bytes 2097152 | tf_op jit(solution)/shard_map/all_to_all | solution.py:177
  603.5 119.6 %all_to_all.41.refs_0_ = bf16[16,5,256,128]{3,2,1,0:T(8,128)(2,1)} all-to-all(bf16[16,5,256,128]{3,2,1,0:T(8,128)(2,1)S(1)} %copy-done.9), channel_id=1, replica_groups=mesh['groups'=2,'seq'=16] {'seq'}, dimensions={0} | all-to-all | bytes 10485760 | tf_op jit(solution)/shard_map/all_to_all | solution.py:177
  723.1 15.6 %shard_map.67 = bf16[4,256,3072]{2,1,0:T(8,128)(2,1)} custom-call(s32[24]{0:T(128)} %select_reduce_fusion.order.before, bf16[16,5,256,128]{3,2,1,0:T(8,128)(2,1)} %all_to_all.41.refs_0_, bf16[16,1,256,128]{3,2,1,0:T(8,128)(2,1)} %all_to_all.40.refs_1_), custom_call_target="tpu_custom_call" | custom-call | tf_op jit(solution)/shard_map/pallas_call | solution.py:188
  (3 shorter events, 0.0 us)
Async XLA Ops:
  30.3 64.3 %all-to-all-start = ((bf16[16,1,3,256,128]{4,3,2,1,0:T(8,128)(2,1)}), bf16[16,1,3,256,128]{4,3,2,1,0:T(8,128)(2,1)}, u32[]{:S(2)}, u32[]{:S(2)}) async-start(bf16[16,1,3,256,128]{4,3,2,1,0:T(8,128)(2,1)} %shard_map.55.before), calls=%async_computation | async-start | bytes 6291456 | tf_op jit(solution)/shard_map/all_to_all | solution.py:136
  39.6 70.1 %copy-start.15 = (s32[24]{0:T(128)S(1)}, s32[24]{0:T(128)}, u32[]{:S(2)}) copy-start(s32[24]{0:T(128)} %select_reduce_fusion.order.before) | copy-start | bytes 292
  39.6 70.8 %copy-start.14 = (bf16[16,1,3,256,128]{4,3,2,1,0:T(8,128)(2,1)S(1)}, bf16[16,1,3,256,128]{4,3,2,1,0:T(8,128)(2,1)}, u32[]{:S(2)}) copy-start(bf16[16,1,3,256,128]{4,3,2,1,0:T(8,128)(2,1)} %shard_map.56.ahead) | copy-start | bytes 9437188
  39.6 70.8 %copy-start.16 = (s32[24]{0:T(128)S(1)}, s32[24]{0:T(128)}, u32[]{:S(2)}) copy-start(s32[24]{0:T(128)} %counts.11) | copy-start | bytes 292
  94.6 117.8 %all-to-all-start.2 = ((bf16[16,1,3,256,128]{4,3,2,1,0:T(8,128)(2,1)}), bf16[16,1,3,256,128]{4,3,2,1,0:T(8,128)(2,1)}, u32[]{:S(2)}, u32[]{:S(2)}) async-start(bf16[16,1,3,256,128]{4,3,2,1,0:T(8,128)(2,1)} %shard_map.56.ahead), calls=%async_computation.2 | async-start | bytes 6291456 | tf_op jit(solution)/shard_map/all_to_all | solution.py:136
  205.1 2.4 copy-start
  212.4 4.7 copy-start.11
  212.4 86.9 %all-to-all-start.1 = ((bf16[16,1,3,256,128]{4,3,2,1,0:T(8,128)(2,1)}), bf16[16,1,3,256,128]{4,3,2,1,0:T(8,128)(2,1)}, u32[]{:S(2)}, u32[]{:S(2)}) async-start(bf16[16,1,3,256,128]{4,3,2,1,0:T(8,128)(2,1)} %shard_map.58.ahead), calls=%async_computation.1 | async-start | bytes 6291456 | tf_op jit(solution)/shard_map/all_to_all | solution.py:136
  217.0 2.5 copy-start.1
  292.0 2.4 copy-start.2
  299.3 6.4 copy-start.12
  299.3 82.9 %all-to-all-start.4 = ((bf16[16,1,3,256,128]{4,3,2,1,0:T(8,128)(2,1)}), bf16[16,1,3,256,128]{4,3,2,1,0:T(8,128)(2,1)}, u32[]{:S(2)}, u32[]{:S(2)}) async-start(bf16[16,1,3,256,128]{4,3,2,1,0:T(8,128)(2,1)} %shard_map.60.ahead), calls=%async_computation.4 | async-start | bytes 6291456 | tf_op jit(solution)/shard_map/all_to_all | solution.py:136
  305.7 2.5 copy-start.3
  375.0 2.4 copy-start.4
  382.2 4.7 copy-start.13
  382.2 64.8 %all-to-all-start.3 = ((bf16[16,1,3,256,128]{4,3,2,1,0:T(8,128)(2,1)}), bf16[16,1,3,256,128]{4,3,2,1,0:T(8,128)(2,1)}, u32[]{:S(2)}, u32[]{:S(2)}) async-start(bf16[16,1,3,256,128]{4,3,2,1,0:T(8,128)(2,1)} %shard_map.62.ahead), calls=%async_computation.3 | async-start | bytes 6291456 | tf_op jit(solution)/shard_map/all_to_all | solution.py:136
  386.9 2.5 copy-start.5
  439.7 2.4 copy-start.6
  447.0 14.8 %copy-start.10 = (bf16[16,1,3,256,128]{4,3,2,1,0:T(8,128)(2,1)S(1)}, bf16[16,1,3,256,128]{4,3,2,1,0:T(8,128)(2,1)}, u32[]{:S(2)}) copy-start(bf16[16,1,3,256,128]{4,3,2,1,0:T(8,128)(2,1)} %shard_map.64.ahead) | copy-start | bytes 9437188
  447.0 74.6 %all-to-all-start.6 = ((bf16[16,1,3,256,128]{4,3,2,1,0:T(8,128)(2,1)}), bf16[16,1,3,256,128]{4,3,2,1,0:T(8,128)(2,1)}, u32[]{:S(2)}, u32[]{:S(2)}) async-start(bf16[16,1,3,256,128]{4,3,2,1,0:T(8,128)(2,1)} %shard_map.64.ahead), calls=%async_computation.6 | async-start | bytes 6291456 | tf_op jit(solution)/shard_map/all_to_all | solution.py:136
  461.8 2.5 copy-start.7
  514.6 2.4 copy-start.8
  521.6 2.5 copy-start.9
